TPU v7x, 32 devices: a whole 2x2x4 slice. The times are simulated.
32 devices in a mesh: leaf: 32 (over z, y, x, core).
Axes of the slice: x: 2, y: 2, z: 4, core: 2. Of those that a mesh axis runs over, the one named last changes fastest.
Arguments:
- white_noise: float32 [32768, 128], P('leaf'), may hold values from -6 to 6
- leaf_inverse: float32 [32768, 1024], P('leaf'), may hold values from -1 to 4, as said below
- bases: float32 [32768, 640], P('leaf'), may hold values from -2 to 2
Outputs:
- solution: float32 [32768, 128], P('leaf')
Inputs may be any that keep to these rules, and one draw needn't show every extreme that they name: `leaf_inverse`: each leaf's block of 1024 rows is symmetric positive definite.
All inputs are finite; a program needn't handle non-finite values.
Results may differ from a plain program's by a relative error of at most 0.0001.
Values sent between devices are 32-bit elements; how exact they have to be, the bound alone decides.
A program may use at most 128 MiB of HBM per device.

v0:
```python
import functools

import jax
import jax.numpy as jnp
from jax import lax
from jax.experimental import pallas as pl
from jax.experimental.pallas import tpu as pltpu
from jax.sharding import PartitionSpec as P

R = 128
PANEL = 16
F32 = jnp.float32
BF16 = jnp.bfloat16


def split2(x):
    high = x.astype(BF16)
    return high, (x - high.astype(F32)).astype(BF16)


def split3(x):
    high = x.astype(BF16)
    rest = x - high.astype(F32)
    mid = rest.astype(BF16)
    return high, mid, (rest - mid.astype(F32)).astype(BF16)


def mxu(a, b, dim):
    return lax.dot_general(a, b, (((dim,), (0,)), ((), ())), preferred_element_type=F32)


def product(a, b, dim=1):
    a_high, a_low = split2(a)
    b_high, b_low = split2(b)
    return mxu(a_high, b_high, dim) + (mxu(a_high, b_low, dim) + mxu(a_low, b_high, dim))


def negative_inverse(work):
    size = work.shape[0]
    row = lax.broadcasted_iota(jnp.int32, (PANEL, size), 0)
    lane = lax.broadcasted_iota(jnp.int32, (PANEL, size), 1)
    whole_row = lax.broadcasted_iota(jnp.int32, (size, size), 0)
    whole_lane = lax.broadcasted_iota(jnp.int32, (size, size), 1)

    def step(block, carry):
        base = pl.multiple_of(block * PANEL, PANEL)
        panel = work[pl.ds(base, PANEL), :]
        columns = [
            jnp.broadcast_to(
                jnp.sum(jnp.where(lane == base + j, panel, 0.0), axis=1, keepdims=True), (PANEL, size)
            )
            for j in range(PANEL)
        ]
        inside = (lane >= base) & (lane < base + PANEL)
        bordered = jnp.where(inside, jnp.where(lane == base + row, -1.0, 0.0), panel)
        reduced = bordered
        scale = jnp.ones((PANEL, size), F32)
        for k in range(PANEL):
            pivot = 1.0 / jnp.broadcast_to(columns[k][k : k + 1], (PANEL, size))
            factor = jnp.where(row == k, 0.0, columns[k] * pivot)
            scale = jnp.where(row == k, pivot, scale)
            for j in range(k + 1, PANEL):
                columns[j] = columns[j] - factor * jnp.broadcast_to(columns[j][k : k + 1], (PANEL, size))
            reduced = reduced - factor * jnp.broadcast_to(reduced[k : k + 1], (PANEL, size))
        a1, a2, a3 = split3(bordered)
        b1, b2, b3 = split3(reduced * scale)
        update = mxu(
            jnp.concatenate([a1, a1, a2, a1, a3, a2], axis=0),
            jnp.concatenate([b1, b2, b1, b3, b1, b2], axis=0),
            0,
        )
        crossed = (whole_row >= base) & (whole_row < base + PANEL)
        crossed |= (whole_lane >= base) & (whole_lane < base + PANEL)
        work[...] = jnp.where(crossed, 0.0, work[...]) - update
        return carry

    lax.fori_loop(0, size // PANEL, step, 0)


def tree_kernel(levels, gram, coefficients, *scratch):
    mine = [gram] + list(scratch[: levels - 1])
    theirs = scratch[levels - 1 : 2 * levels - 1]
    weights = scratch[2 * levels - 1 : 3 * levels - 1]
    work, send_sem, recv_sem = scratch[3 * levels - 1 :]
    me = lax.axis_index("leaf")
    partners = [me + 2**l * (1 - 2 * ((me // 2**l) % 2)) for l in range(levels)]

    barrier = pltpu.get_barrier_semaphore()
    for partner in partners:
        pl.semaphore_signal(barrier, inc=1, device_id=(partner,), device_id_type=pl.DeviceIdType.MESH)
    pl.semaphore_wait(barrier, levels)

    used = 0
    copies = [[] for _ in range(levels)]

    def send(level, rows, columns):
        nonlocal used
        copy = pltpu.make_async_remote_copy(
            src_ref=mine[level].at[rows, columns],
            dst_ref=theirs[level].at[rows, columns],
            send_sem=send_sem.at[used],
            recv_sem=recv_sem.at[used],
            device_id=(partners[level],),
            device_id_type=pl.DeviceIdType.MESH,
        )
        used += 1
        copy.start()
        copies[level].append(copy)

    def send_row(level, m):
        end = (levels - level + 1) * R
        rows = slice(m * R, (m + 1) * R)
        if m == 0:
            send(level, rows, slice(0, R))
            send(level, rows, slice(R, end))
        else:
            send(level, rows, slice(m * R, end))

    for m in range(levels):
        send_row(0, m)
    eye = (
        lax.broadcasted_iota(jnp.int32, (R, R), 0) == lax.broadcasted_iota(jnp.int32, (R, R), 1)
    ).astype(F32)
    for level in range(levels):
        left = levels - level
        end = (left + 1) * R
        copies[level][0].wait_recv()
        work[...] = eye + (mine[level][0:R, 0:R] + theirs[level][0:R, 0:R])
        negative_inverse(work)
        copies[level][1].wait_recv()
        rest = mine[level][0:R, R:end] + theirs[level][0:R, R:end]
        theirs[level][0:R, R:end] = rest
        weights[level][...] = product(-work[...], rest)
        for m in range(1, left):
            copies[level][m + 1].wait_recv()
            rows = slice(m * R, (m + 1) * R)
            mine[level + 1][(m - 1) * R : m * R, (m - 1) * R : end - R] = (
                mine[level][rows, m * R : end] + theirs[level][rows, m * R : end]
            ) - product(theirs[level][0:R, rows], weights[level][:, (m - 1) * R : end - R], 0)
            send_row(level + 1, m - 1)
    for level in reversed(range(levels)):
        left = levels - level
        part = weights[level][:, (left - 1) * R :]
        if level < levels - 1:
            part = part - product(weights[level][:, : (left - 1) * R], coefficients[(level + 1) * R :, :])
        coefficients[level * R : (level + 1) * R, :] = part
    for level in range(levels):
        for copy in copies[level]:
            copy.wait_send()


def tree(gram):
    levels = gram.shape[0] // R
    shapes = [((levels - l) * R, (levels - l + 1) * R) for l in range(levels)]
    count = sum(levels - l + 1 for l in range(levels))
    vmem = pl.BlockSpec(memory_space=pltpu.VMEM)
    return pl.pallas_call(
        functools.partial(tree_kernel, levels),
        out_shape=jax.ShapeDtypeStruct((levels * R, R), F32),
        in_specs=[vmem],
        out_specs=vmem,
        scratch_shapes=[pltpu.VMEM(s, F32) for s in shapes[1:]]
        + [pltpu.VMEM(s, F32) for s in shapes]
        + [pltpu.VMEM((R, s[0]), F32) for s in shapes]
        + [
            pltpu.VMEM((R, R), F32),
            pltpu.SemaphoreType.DMA((count,)),
            pltpu.SemaphoreType.DMA((count,)),
        ],
        compiler_params=pltpu.CompilerParams(
            collective_id=0, has_side_effects=True, vmem_limit_bytes=56 * 2**20
        ),
    )(gram)


def body(white_noise, leaf_inverse, bases):
    split = bases.shape[1]
    right_side = jnp.concatenate([bases, white_noise], axis=1)
    solved = jnp.dot(leaf_inverse, right_side, precision=lax.Precision.HIGH, preferred_element_type=F32)
    gram = lax.dot_general(
        bases, solved, (((0,), (0,)), ((), ())), precision=lax.Precision.HIGH, preferred_element_type=F32
    )
    coefficients = tree(gram)
    return solved[:, split:] - jnp.dot(
        solved[:, :split], coefficients, precision=lax.Precision.HIGH, preferred_element_type=F32
    )


def solution(mesh):
    in_specs = (P("leaf", None), P("leaf", None), P("leaf", None))
    out_specs = P("leaf", None)
    return jax.shard_map(body, mesh=mesh, in_specs=in_specs, out_specs=out_specs, check_vma=False)
```

profile of v0, /device:TPU:0, one launch (start us, length us, event | category | flops | bytes accessed | tf_op | source)
XLA Modules:
  0.0 79.8 jit_solution(9173837297290659294)
XLA Ops:
  0.0 0.0 copy-start
  0.0 13.4 %fusion = f32[768,1024]{1,0:T(8,128)S(1)} fusion(f32[1024,1024]{1,0:T(8,128)} %param.4, f32[1024,128]{1,0:T(8,128)} %param.3, f32[1024,640]{1,0:T(8,128)} %param.5), kind=kOutput, calls=%fused_computation | convolution fusion | flops 4832624640 | bytes 10485760 | tf_op jit(solution)/shard_map/dot_general | solution.py:179
  13.4 0.0 copy-done
  13.4 5.1 %convolution_bitcast_fusion.gram = f32[640,768]{1,0:T(8,128)} fusion(f32[768,1024]{1,0:T(8,128)S(1)} %fusion, f32[1024,640]{1,0:T(8,128)S(1)} %copy-done), kind=kOutput, calls=%fused_computation.6 | convolution fusion | flops 3019898880 | bytes 7733248 | tf_op jit(solution)/shard_map/dot_general | solution.py:180
  18.5 58.4 %shard_map.37 = f32[640,128]{1,0:T(8,128)} custom-call(f32[640,768]{1,0:T(8,128)} %convolution_bitcast_fusion.gram), custom_call_target="tpu_custom_call" | custom-call | tf_op jit(solution)/shard_map/pallas_call | solution.py:157
  76.9 1.9 %fusion.6 = f32[1024,128]{0,1:T(8,128)S(1)} fusion(f32[640,128]{1,0:T(8,128)} %shard_map.37, f32[1024,768]{0,1:T(8,128)S(1)} %bitcast.7), kind=kOutput, calls=%fused_computation.7 | convolution fusion | flops 503447552 | bytes 3997696 | tf_op jit(solution)/shard_map/dot_general | solution.py:184
  78.8 1.0 %copy.5 = f32[1024,128]{1,0:T(8,128)} copy(f32[1024,128]{0,1:T(8,128)S(1)} %fusion.6) | data formatting | bytes 1048576 | tf_op jit(solution)/shard_map/sub | solution.py:184
Async XLA Ops:
  0.0 13.4 %copy-start = (f32[1024,640]{1,0:T(8,128)S(1)}, f32[1024,640]{1,0:T(8,128)}, u32[]{:S(2)}) copy-start(f32[1024,640]{1,0:T(8,128)} %param.5) | copy-start | bytes 7864324
where the time goes:
time: 79.9 us; the launch traced here: 79.8 us
  Pallas kernels  58.4 us (73%)
  matrix products  20.3 us (25%)
  local copies, waits for them, and re-layouts  1 us (1%)
    pallas_call x1, Pallas kernels, tree(): pl.pallas_call(functools.partial(tree_kernel, levels), out_shape=jax.Shap...  58.4 us
    dot_general x1, matrix products, body(): jnp.dot(leaf_inverse, right_side, precision=lax.Precision.HIGH, preferred...  13.4 us
    dot_general x1, matrix products, body(): lax.dot_general(bases, solved, (((0,), (0,)), ((), ())), precision=lax.Pr...  5.08 us
    dot_general x1, matrix products, body(): jnp.dot(solved[:, :split], coefficients, precision=lax.Precision.HIGH, pr...  1.87 us

commit v1 on v0

--- a/solution.py
+++ b/solution.py
@@ -35,7 +35,7 @@
     return mxu(a_high, b_high, dim) + (mxu(a_high, b_low, dim) + mxu(a_low, b_high, dim))
 
 
-def negative_inverse(work):
+def negative_inverse(work, between):
     size = work.shape[0]
     row = lax.broadcasted_iota(jnp.int32, (PANEL, size), 0)
     lane = lax.broadcasted_iota(jnp.int32, (PANEL, size), 1)
@@ -74,47 +74,66 @@
         work[...] = jnp.where(crossed, 0.0, work[...]) - update
         return carry
 
-    lax.fori_loop(0, size // PANEL, step, 0)
+    steps = size // PANEL
+    early = steps * 3 // 4
+    lax.fori_loop(0, early, step, 0)
+    between()
+    lax.fori_loop(early, steps, step, 0)
 
 
 def tree_kernel(levels, gram, coefficients, *scratch):
     mine = [gram] + list(scratch[: levels - 1])
     theirs = scratch[levels - 1 : 2 * levels - 1]
     weights = scratch[2 * levels - 1 : 3 * levels - 1]
-    work, send_sem, recv_sem = scratch[3 * levels - 1 :]
+    rest, work, send_sem, recv_sem = scratch[3 * levels - 1 :]
     me = lax.axis_index("leaf")
     partners = [me + 2**l * (1 - 2 * ((me // 2**l) % 2)) for l in range(levels)]
+    half = R // 2
+    offset = (me % 2) * half
 
     barrier = pltpu.get_barrier_semaphore()
     for partner in partners:
         pl.semaphore_signal(barrier, inc=1, device_id=(partner,), device_id_type=pl.DeviceIdType.MESH)
     pl.semaphore_wait(barrier, levels)
 
-    used = 0
-    copies = [[] for _ in range(levels)]
-
-    def send(level, rows, columns):
-        nonlocal used
+    started = []
+    direct, passed = {}, {}
+
+    def start(source, target, partner):
         copy = pltpu.make_async_remote_copy(
-            src_ref=mine[level].at[rows, columns],
-            dst_ref=theirs[level].at[rows, columns],
-            send_sem=send_sem.at[used],
-            recv_sem=recv_sem.at[used],
-            device_id=(partners[level],),
+            src_ref=source,
+            dst_ref=target,
+            send_sem=send_sem.at[len(started)],
+            recv_sem=recv_sem.at[len(started)],
+            device_id=(partner,),
             device_id_type=pl.DeviceIdType.MESH,
         )
-        used += 1
         copy.start()
-        copies[level].append(copy)
+        started.append(copy)
+        return copy
+
+    def part(level, m):
+        columns = slice(max(m, 1) * R, (levels - level + 1) * R)
+        if level == 0:
+            return slice(m * R, (m + 1) * R), columns
+        return pl.ds(pl.multiple_of(m * R + offset, half), half), columns
 
     def send_row(level, m):
-        end = (levels - level + 1) * R
-        rows = slice(m * R, (m + 1) * R)
         if m == 0:
-            send(level, rows, slice(0, R))
-            send(level, rows, slice(R, end))
-        else:
-            send(level, rows, slice(m * R, end))
+            corner = (slice(0, R), slice(0, R))
+            direct[level, -1] = start(mine[level].at[corner], theirs[level].at[corner], partners[level])
+        where = part(level, m)
+        direct[level, m] = start(mine[level].at[where], theirs[level].at[where], partners[level])
+
+    def pass_on(level, m):
+        direct[level, m].wait_recv()
+        if level > 0:
+            where = part(level, m)
+            passed[level, m] = start(theirs[level].at[where], theirs[level].at[where], partners[0])
+
+    def arrived(level, m):
+        if level > 0:
+            passed[level, m].wait_recv()
 
     for m in range(levels):
         send_row(0, m)
@@ -124,35 +143,43 @@
     for level in range(levels):
         left = levels - level
         end = (left + 1) * R
-        copies[level][0].wait_recv()
-        work[...] = eye + (mine[level][0:R, 0:R] + theirs[level][0:R, 0:R])
-        negative_inverse(work)
-        copies[level][1].wait_recv()
-        rest = mine[level][0:R, R:end] + theirs[level][0:R, R:end]
-        theirs[level][0:R, R:end] = rest
-        weights[level][...] = product(-work[...], rest)
-        for m in range(1, left):
-            copies[level][m + 1].wait_recv()
+
+        def update(m):
+            arrived(level, m)
             rows = slice(m * R, (m + 1) * R)
             mine[level + 1][(m - 1) * R : m * R, (m - 1) * R : end - R] = (
                 mine[level][rows, m * R : end] + theirs[level][rows, m * R : end]
-            ) - product(theirs[level][0:R, rows], weights[level][:, (m - 1) * R : end - R], 0)
+            ) - product(rest[:, (m - 1) * R : m * R], weights[level][:, (m - 1) * R : end - R], 0)
             send_row(level + 1, m - 1)
+
+        direct[level, -1].wait_recv()
+        work[...] = eye + (mine[level][0:R, 0:R] + theirs[level][0:R, 0:R])
+        negative_inverse(work, functools.partial(pass_on, level, 0))
+        if left > 1:
+            pass_on(level, 1)
+        arrived(level, 0)
+        rest[:, : end - R] = mine[level][0:R, R:end] + theirs[level][0:R, R:end]
+        weights[level][...] = product(-work[...], rest[:, : end - R])
+        if left > 1:
+            update(1)
+        for m in range(2, left):
+            pass_on(level, m)
+        for m in range(2, left):
+            update(m)
     for level in reversed(range(levels)):
         left = levels - level
-        part = weights[level][:, (left - 1) * R :]
+        column = weights[level][:, (left - 1) * R :]
         if level < levels - 1:
-            part = part - product(weights[level][:, : (left - 1) * R], coefficients[(level + 1) * R :, :])
-        coefficients[level * R : (level + 1) * R, :] = part
-    for level in range(levels):
-        for copy in copies[level]:
-            copy.wait_send()
+            column = column - product(weights[level][:, : (left - 1) * R], coefficients[(level + 1) * R :, :])
+        coefficients[level * R : (level + 1) * R, :] = column
+    for copy in started:
+        copy.wait_send()
 
 
 def tree(gram):
     levels = gram.shape[0] // R
     shapes = [((levels - l) * R, (levels - l + 1) * R) for l in range(levels)]
-    count = sum(levels - l + 1 for l in range(levels))
+    count = sum((levels - l) * (2 if l else 1) + 1 for l in range(levels))
     vmem = pl.BlockSpec(memory_space=pltpu.VMEM)
     return pl.pallas_call(
         functools.partial(tree_kernel, levels),
@@ -163,6 +190,7 @@
         + [pltpu.VMEM(s, F32) for s in shapes]
         + [pltpu.VMEM((R, s[0]), F32) for s in shapes]
         + [
+            pltpu.VMEM((R, levels * R), F32),
             pltpu.VMEM((R, R), F32),
             pltpu.SemaphoreType.DMA((count,)),
             pltpu.SemaphoreType.DMA((count,)),
@@ -173,13 +201,58 @@
     )(gram)
 
 
+def leaf_kernel(inverse, bases, noise, solved, gram, high, low):
+    tile = inverse.shape[0]
+    split = bases.shape[1]
+    levels = split // R
+    step = pl.program_id(0)
+
+    @pl.when(step == 0)
+    def _():
+        for ref, columns in ((bases, slice(0, split)), (noise, slice(split, split + noise.shape[1]))):
+            high[:, columns], low[:, columns] = split2(ref[...])
+        gram[...] = jnp.zeros_like(gram)
+
+    a_high, a_low = split2(inverse[...])
+    found = mxu(a_high, high[...], 1) + (mxu(a_high, low[...], 1) + mxu(a_low, high[...], 1))
+    solved[...] = found
+    s_high, s_low = split2(found)
+    rows = pl.ds(pl.multiple_of(step * tile, tile), tile)
+    for m in range(levels):
+        b_high = high[rows, m * R : (m + 1) * R]
+        b_low = low[rows, m * R : (m + 1) * R]
+        c_high, c_low = s_high[:, m * R :], s_low[:, m * R :]
+        gram[m * R : (m + 1) * R, m * R :] += mxu(b_high, c_high, 0) + (
+            mxu(b_high, c_low, 0) + mxu(b_low, c_high, 0)
+        )
+
+
+def leaf(leaf_inverse, bases, noise):
+    cells, split = bases.shape
+    width = split + noise.shape[1]
+    tile = min(cells, 256)
+    whole = lambda i: (0, 0)
+    return pl.pallas_call(
+        leaf_kernel,
+        grid=(cells // tile,),
+        out_shape=(
+            jax.ShapeDtypeStruct((cells, width), F32),
+            jax.ShapeDtypeStruct((split, width), F32),
+        ),
+        in_specs=[
+            pl.BlockSpec((tile, cells), lambda i: (i, 0)),
+            pl.BlockSpec(bases.shape, whole),
+            pl.BlockSpec(noise.shape, whole),
+        ],
+        out_specs=(pl.BlockSpec((tile, width), lambda i: (i, 0)), pl.BlockSpec((split, width), whole)),
+        scratch_shapes=[pltpu.VMEM((cells, width), BF16), pltpu.VMEM((cells, width), BF16)],
+        compiler_params=pltpu.CompilerParams(vmem_limit_bytes=56 * 2**20),
+    )(leaf_inverse, bases, noise)
+
+
 def body(white_noise, leaf_inverse, bases):
     split = bases.shape[1]
-    right_side = jnp.concatenate([bases, white_noise], axis=1)
-    solved = jnp.dot(leaf_inverse, right_side, precision=lax.Precision.HIGH, preferred_element_type=F32)
-    gram = lax.dot_general(
-        bases, solved, (((0,), (0,)), ((), ())), precision=lax.Precision.HIGH, preferred_element_type=F32
-    )
+    solved, gram = leaf(leaf_inverse, bases, white_noise)
     coefficients = tree(gram)
     return solved[:, split:] - jnp.dot(
         solved[:, :split], coefficients, precision=lax.Precision.HIGH, preferred_element_type=F32

time: 79.9 us -> 69.5 us (0.87)
  matrix products: 20.3 us -> 3.89 us
  Pallas kernels: 58.4 us -> 65.5 us
  local copies, waits for them, and re-layouts: 1 us -> 0 us
    dot_general x2 -> x0, matrix products: 18.5 us -> none  [the longest x1 13.4 us: body(): jnp.dot(leaf_inverse, right_side, precision=lax.Precision.HIGH, preferred...]
    pallas_call x0 -> x1, Pallas kernels: none -> 15.1 us  [leaf(): pl.pallas_call(leaf_kernel, grid=(cells // tile,), out_shape=(jax.ShapeDt...]
    pallas_call x1, Pallas kernels: 58.4 us -> 50.4 us  [tree(): pl.pallas_call(functools.partial(tree_kernel, levels), out_shape=jax.Shap...]
    dot_general x1, matrix products: 1.87 us -> 3.89 us  [body(): jnp.dot(solved[:, :split], coefficients, precision=lax.Precision.HIGH, pr...]
    sub x1 -> x0, local copies, waits for them, and re-layouts: 1 us -> none  [body(): solved[:, split:]]
where the time goes in v1:
time: 69.5 us; the launch traced here: 69.4 us
  Pallas kernels  65.5 us (94%)
  matrix products  3.89 us (6%)
    pallas_call x1, Pallas kernels, tree(): pl.pallas_call(functools.partial(tree_kernel, levels), out_shape=jax.Shap...  50.4 us
    pallas_call x1, Pallas kernels, leaf(): pl.pallas_call(leaf_kernel, grid=(cells // tile,), out_shape=(jax.ShapeDt...  15.1 us
    dot_general x1, matrix products, body(): jnp.dot(solved[:, :split], coefficients, precision=lax.Precision.HIGH, pr...  3.89 us

profile of v1, /device:TPU:0, one launch (start us, length us, event | category | flops | bytes accessed | tf_op | source)
XLA Modules:
  0.0 69.4 jit_solution(6277403284638803995)
XLA Ops:
  0.0 15.1 %shard_map.37 = (f32[1024,768]{1,0:T(8,128)}, f32[640,768]{1,0:T(8,128)}) custom-call(f32[1024,1024]{1,0:T(8,128)} %inverse.1, f32[1024,640]{1,0:T(8,128)} %bases.1, f32[1024,128]{1,0:T(8,128)} %noise.1), custom_call_target="tpu_custom_call" | custom-call | tf_op jit(solution)/shard_map/pallas_call | solution.py:235
  15.1 50.4 %shard_map.38 = f32[640,128]{1,0:T(8,128)} custom-call(f32[640,768]{1,0:T(8,128)} %get-tuple-element.8.gram), custom_call_target="tpu_custom_call" | custom-call | tf_op jit(solution)/shard_map/pallas_call | solution.py:184
  65.5 3.9 %fusion.2 = f32[1024,128]{1,0:T(8,128)} fusion(f32[640,128]{1,0:T(8,128)} %shard_map.38, f32[1024,768]{1,0:T(8,128)} %get-tuple-element.7), kind=kOutput, calls=%fused_computation.2 | convolution fusion | flops 503447552 | bytes 3997696 | tf_op jit(solution)/shard_map/dot_general | solution.py:257

commit v2 on v1

--- a/solution.py
+++ b/solution.py
@@ -81,11 +81,37 @@
     lax.fori_loop(early, steps, step, 0)
 
 
-def tree_kernel(levels, gram, coefficients, *scratch):
-    mine = [gram] + list(scratch[: levels - 1])
-    theirs = scratch[levels - 1 : 2 * levels - 1]
-    weights = scratch[2 * levels - 1 : 3 * levels - 1]
-    rest, work, send_sem, recv_sem = scratch[3 * levels - 1 :]
+def leaf_products(inverse, bases, noise, turned_high, turned_low, high, low, noise_solved, gram):
+    cells, split = bases.shape
+    width = split + noise.shape[1]
+    for start in range(0, width, 2 * R):
+        stop = min(start + 2 * R, width)
+        pieces = [bases[:, start : min(stop, split)]] if start < split else []
+        if stop > split:
+            pieces.append(noise[:, max(start, split) - split : stop - split])
+        r_high, r_low = split2(jnp.concatenate(pieces, axis=1))
+        a_high, a_low = split2(inverse[...])
+        found = mxu(a_high, r_high, 1) + (mxu(a_high, r_low, 1) + mxu(a_low, r_high, 1))
+        inner = min(stop, split)
+        if start < split:
+            fresh = slice(start, inner)
+            turned_high[fresh, :], turned_low[fresh, :] = split2(bases[:, fresh].T)
+        s_high, s_low = split2(found)
+        if start < split:
+            high[:, fresh], low[:, fresh] = s_high[:, : inner - start], s_low[:, : inner - start]
+        if stop > split:
+            noise_solved[:, max(start, split) - split : stop - split] = found[:, max(start, split) - start :]
+        b_high = turned_high[:inner, :]
+        gram[:inner, start:stop] = mxu(b_high, s_high, 1) + (
+            mxu(b_high, s_low, 1) + mxu(turned_low[:inner, :], s_high, 1)
+        )
+
+
+def tree_kernel(levels, noise, inverse, bases, solution_ref, *scratch):
+    mine = scratch[:levels]
+    theirs = scratch[levels : 2 * levels]
+    high, low, turned_high, turned_low, weights, rest, work, send_sem, recv_sem = scratch[2 * levels :]
+    split = levels * R
     me = lax.axis_index("leaf")
     partners = [me + 2**l * (1 - 2 * ((me // 2**l) % 2)) for l in range(levels)]
     half = R // 2
@@ -94,6 +120,7 @@
     barrier = pltpu.get_barrier_semaphore()
     for partner in partners:
         pl.semaphore_signal(barrier, inc=1, device_id=(partner,), device_id_type=pl.DeviceIdType.MESH)
+    leaf_products(inverse, bases, noise, turned_high, turned_low, high, low, solution_ref, mine[0])
     pl.semaphore_wait(barrier, levels)
 
     started = []
@@ -143,13 +170,15 @@
     for level in range(levels):
         left = levels - level
         end = (left + 1) * R
+        here = slice(level * R, (level + 1) * R)
+        later = (level + 1) * R
 
         def update(m):
             arrived(level, m)
             rows = slice(m * R, (m + 1) * R)
             mine[level + 1][(m - 1) * R : m * R, (m - 1) * R : end - R] = (
                 mine[level][rows, m * R : end] + theirs[level][rows, m * R : end]
-            ) - product(rest[:, (m - 1) * R : m * R], weights[level][:, (m - 1) * R : end - R], 0)
+            ) - product(rest[:, (m - 1) * R : m * R], weights[here, (level + m) * R :], 0)
             send_row(level + 1, m - 1)
 
         direct[level, -1].wait_recv()
@@ -159,104 +188,53 @@
             pass_on(level, 1)
         arrived(level, 0)
         rest[:, : end - R] = mine[level][0:R, R:end] + theirs[level][0:R, R:end]
-        weights[level][...] = product(-work[...], rest[:, : end - R])
+        weights[here, later:] = product(-work[...], rest[:, : end - R])
         if left > 1:
             update(1)
         for m in range(2, left):
             pass_on(level, m)
         for m in range(2, left):
             update(m)
-    for level in reversed(range(levels)):
-        left = levels - level
-        column = weights[level][:, (left - 1) * R :]
-        if level < levels - 1:
-            column = column - product(weights[level][:, : (left - 1) * R], coefficients[(level + 1) * R :, :])
-        coefficients[level * R : (level + 1) * R, :] = column
+        if level > 0:
+            above = slice(0, level * R)
+            weights[above, later:] = weights[above, later:] - product(
+                weights[above, here], weights[here, later:]
+            )
+    w_high, w_low = split2(weights[:, split:])
+    solution_ref[...] = solution_ref[...] - (
+        mxu(high[...], w_high, 1) + (mxu(high[...], w_low, 1) + mxu(low[...], w_high, 1))
+    )
     for copy in started:
         copy.wait_send()
 
 
-def tree(gram):
-    levels = gram.shape[0] // R
+def body(white_noise, leaf_inverse, bases):
+    cells, split = bases.shape
+    levels = split // R
     shapes = [((levels - l) * R, (levels - l + 1) * R) for l in range(levels)]
     count = sum((levels - l) * (2 if l else 1) + 1 for l in range(levels))
     vmem = pl.BlockSpec(memory_space=pltpu.VMEM)
     return pl.pallas_call(
         functools.partial(tree_kernel, levels),
-        out_shape=jax.ShapeDtypeStruct((levels * R, R), F32),
-        in_specs=[vmem],
+        out_shape=jax.ShapeDtypeStruct(white_noise.shape, F32),
+        in_specs=[vmem] * 3,
         out_specs=vmem,
-        scratch_shapes=[pltpu.VMEM(s, F32) for s in shapes[1:]]
-        + [pltpu.VMEM(s, F32) for s in shapes]
-        + [pltpu.VMEM((R, s[0]), F32) for s in shapes]
+        scratch_shapes=[pltpu.VMEM(s, F32) for s in shapes + shapes]
         + [
-            pltpu.VMEM((R, levels * R), F32),
+            pltpu.VMEM((cells, split), BF16),
+            pltpu.VMEM((cells, split), BF16),
+            pltpu.VMEM((split, cells), BF16),
+            pltpu.VMEM((split, cells), BF16),
+            pltpu.VMEM(shapes[0], F32),
+            pltpu.VMEM((R, split), F32),
             pltpu.VMEM((R, R), F32),
             pltpu.SemaphoreType.DMA((count,)),
             pltpu.SemaphoreType.DMA((count,)),
         ],
         compiler_params=pltpu.CompilerParams(
-            collective_id=0, has_side_effects=True, vmem_limit_bytes=56 * 2**20
+            collective_id=0, has_side_effects=True, vmem_limit_bytes=60 * 2**20
         ),
-    )(gram)
-
-
-def leaf_kernel(inverse, bases, noise, solved, gram, high, low):
-    tile = inverse.shape[0]
-    split = bases.shape[1]
-    levels = split // R
-    step = pl.program_id(0)
-
-    @pl.when(step == 0)
-    def _():
-        for ref, columns in ((bases, slice(0, split)), (noise, slice(split, split + noise.shape[1]))):
-            high[:, columns], low[:, columns] = split2(ref[...])
-        gram[...] = jnp.zeros_like(gram)
-
-    a_high, a_low = split2(inverse[...])
-    found = mxu(a_high, high[...], 1) + (mxu(a_high, low[...], 1) + mxu(a_low, high[...], 1))
-    solved[...] = found
-    s_high, s_low = split2(found)
-    rows = pl.ds(pl.multiple_of(step * tile, tile), tile)
-    for m in range(levels):
-        b_high = high[rows, m * R : (m + 1) * R]
-        b_low = low[rows, m * R : (m + 1) * R]
-        c_high, c_low = s_high[:, m * R :], s_low[:, m * R :]
-        gram[m * R : (m + 1) * R, m * R :] += mxu(b_high, c_high, 0) + (
-            mxu(b_high, c_low, 0) + mxu(b_low, c_high, 0)
-        )
-
-
-def leaf(leaf_inverse, bases, noise):
-    cells, split = bases.shape
-    width = split + noise.shape[1]
-    tile = min(cells, 256)
-    whole = lambda i: (0, 0)
-    return pl.pallas_call(
-        leaf_kernel,
-        grid=(cells // tile,),
-        out_shape=(
-            jax.ShapeDtypeStruct((cells, width), F32),
-            jax.ShapeDtypeStruct((split, width), F32),
-        ),
-        in_specs=[
-            pl.BlockSpec((tile, cells), lambda i: (i, 0)),
-            pl.BlockSpec(bases.shape, whole),
-            pl.BlockSpec(noise.shape, whole),
-        ],
-        out_specs=(pl.BlockSpec((tile, width), lambda i: (i, 0)), pl.BlockSpec((split, width), whole)),
-        scratch_shapes=[pltpu.VMEM((cells, width), BF16), pltpu.VMEM((cells, width), BF16)],
-        compiler_params=pltpu.CompilerParams(vmem_limit_bytes=56 * 2**20),
-    )(leaf_inverse, bases, noise)
-
-
-def body(white_noise, leaf_inverse, bases):
-    split = bases.shape[1]
-    solved, gram = leaf(leaf_inverse, bases, white_noise)
-    coefficients = tree(gram)
-    return solved[:, split:] - jnp.dot(
-        solved[:, :split], coefficients, precision=lax.Precision.HIGH, preferred_element_type=F32
-    )
+    )(white_noise, leaf_inverse, bases)
 
 
 def solution(mesh):

time: 69.5 us -> 66.1 us (0.951)
  matrix products: 3.89 us -> 0 us
  local copies, waits for them, and re-layouts: 0 us -> 1.87 us
  Pallas kernels: 65.5 us -> 64.1 us
    dot_general x1 -> x0, matrix products: 3.89 us -> none  [body(): jnp.dot(solved[:, :split], coefficients, precision=lax.Precision.HIGH, pr...]
    unnamed x0 -> x1, local copies, waits for them, and re-layouts: none -> 1.87 us
    pallas_call x2 -> x1, Pallas kernels: 65.5 us -> 64.1 us  [body(): pl.pallas_call(functools.partial(tree_kernel, levels), out_shape=jax.Shap...]
where the time goes in v2:
time: 66.1 us; the launch traced here: 66 us
  Pallas kernels  64.1 us (97%)
  local copies, waits for them, and re-layouts  1.87 us (3%)
    pallas_call x1, Pallas kernels, body(): pl.pallas_call(functools.partial(tree_kernel, levels), out_shape=jax.Shap...  64.1 us
    unnamed x1, local copies, waits for them, and re-layouts  1.87 us

profile of v2, /device:TPU:0, one launch (start us, length us, event | category | flops | bytes accessed | tf_op | source)
XLA Modules:
  0.0 66.0 jit_solution(4922683693119394559)
XLA Ops:
  0.0 64.1 %shard_map.37 = f32[1024,128]{1,0:T(8,128)} custom-call(f32[1024,128]{1,0:T(8,128)} %noise.1, f32[1024,1024]{1,0:T(8,128)} %inverse.1, f32[1024,640]{1,0:T(8,128)} %bases.1), custom_call_target="tpu_custom_call" | custom-call | tf_op jit(solution)/shard_map/pallas_call | solution.py:217
  64.1 1.9 %copy.5 = f32[1024,128]{1,0:T(8,128)} copy(f32[1024,128]{1,0:T(8,128)} %shard_map.37) | data formatting | bytes 1048576

commit v3 on v2

--- a/solution.py
+++ b/solution.py
@@ -81,7 +81,7 @@
     lax.fori_loop(early, steps, step, 0)
 
 
-def leaf_products(inverse, bases, noise, turned_high, turned_low, high, low, noise_solved, gram):
+def leaf_products(inverse, bases, noise, turned_high, turned_low, high, low, noise_solved, gram, corner_done):
     cells, split = bases.shape
     width = split + noise.shape[1]
     for start in range(0, width, 2 * R):
@@ -105,6 +105,8 @@
         gram[:inner, start:stop] = mxu(b_high, s_high, 1) + (
             mxu(b_high, s_low, 1) + mxu(turned_low[:inner, :], s_high, 1)
         )
+        if start == 0:
+            corner_done()
 
 
 def tree_kernel(levels, noise, inverse, bases, solution_ref, *scratch):
@@ -120,9 +122,6 @@
     barrier = pltpu.get_barrier_semaphore()
     for partner in partners:
         pl.semaphore_signal(barrier, inc=1, device_id=(partner,), device_id_type=pl.DeviceIdType.MESH)
-    leaf_products(inverse, bases, noise, turned_high, turned_low, high, low, solution_ref, mine[0])
-    pl.semaphore_wait(barrier, levels)
-
     started = []
     direct, passed = {}, {}
 
@@ -145,10 +144,11 @@
             return slice(m * R, (m + 1) * R), columns
         return pl.ds(pl.multiple_of(m * R + offset, half), half), columns
 
+    def send_corner(level):
+        corner = (slice(0, R), slice(0, R))
+        direct[level, -1] = start(mine[level].at[corner], theirs[level].at[corner], partners[level])
+
     def send_row(level, m):
-        if m == 0:
-            corner = (slice(0, R), slice(0, R))
-            direct[level, -1] = start(mine[level].at[corner], theirs[level].at[corner], partners[level])
         where = part(level, m)
         direct[level, m] = start(mine[level].at[where], theirs[level].at[where], partners[level])
 
@@ -162,6 +162,13 @@
         if level > 0:
             passed[level, m].wait_recv()
 
+    def corner_done():
+        pl.semaphore_wait(barrier, levels)
+        send_corner(0)
+
+    leaf_products(
+        inverse, bases, noise, turned_high, turned_low, high, low, solution_ref, mine[0], corner_done
+    )
     for m in range(levels):
         send_row(0, m)
     eye = (
@@ -179,6 +186,8 @@
             mine[level + 1][(m - 1) * R : m * R, (m - 1) * R : end - R] = (
                 mine[level][rows, m * R : end] + theirs[level][rows, m * R : end]
             ) - product(rest[:, (m - 1) * R : m * R], weights[here, (level + m) * R :], 0)
+            if m == 1:
+                send_corner(level + 1)
             send_row(level + 1, m - 1)
 
         direct[level, -1].wait_recv()

time: 66.1 us -> 65.8 us (level)
  no operation moved by 1% of the time
where the time goes in v3:
time: 65.8 us; the launch traced here: 65.6 us
  Pallas kernels  63.8 us (97%)
  local copies, waits for them, and re-layouts  1.87 us (3%)
    pallas_call x1, Pallas kernels, body(): pl.pallas_call(functools.partial(tree_kernel, levels), out_shape=jax.Shap...  63.8 us
    unnamed x1, local copies, waits for them, and re-layouts  1.87 us

profile of v3, /device:TPU:0, one launch (start us, length us, event | category | flops | bytes accessed | tf_op | source)
XLA Modules:
  0.0 65.6 jit_solution(1805218116621370135)
XLA Ops:
  0.0 63.8 %shard_map.37 = f32[1024,128]{1,0:T(8,128)} custom-call(f32[1024,128]{1,0:T(8,128)} %noise.1, f32[1024,1024]{1,0:T(8,128)} %inverse.1, f32[1024,640]{1,0:T(8,128)} %bases.1), custom_call_target="tpu_custom_call" | custom-call | tf_op jit(solution)/shard_map/pallas_call | solution.py:226
  63.8 1.9 %copy.5 = f32[1024,128]{1,0:T(8,128)} copy(f32[1024,128]{1,0:T(8,128)} %shard_map.37) | data formatting | bytes 1048576
